TPU v7x, 256 devices: a whole 4x4x8 slice. The times are simulated.
256 devices in a mesh: row: 8 (over y_hi, x), col: 32 (over y_lo, z, core).
Axes of the slice: x: 4, y: 4 (y_hi: 2, y_lo: 2; y = y_hi * 2 + y_lo), z: 8, core: 2. Of those that a mesh axis runs over, the one named last changes fastest.
Arguments:
- intensity: float32 [16, 2048, 2048], P(None, 'row', 'col'), may hold values from -6 to 6
- punch_radius: int32 [2, 129, 129], replicated, may hold values from 0 to 12
Outputs:
- out_re: float32 [16, 2048, 2048], P(None, ('row', 'col'))
- out_im: float32 [16, 2048, 2048], P(None, ('row', 'col'))
Inputs may be any that keep to these rules, and one draw needn't show every extreme that they name: `punch_radius`: squared radius in voxels; 0 leaves a node unpunched.
All inputs are finite; a program needn't handle non-finite values.
Results may differ from a plain program's by a relative error of at most 0.0029.
Values may be sent and summed in bfloat16 or wider, within the bound.
No kernel may reach another device: no remote copies, remote signals or barrier semaphores. Data moves between devices by JAX's collectives and lax.ppermute only.
A program may use at most 128 MiB of HBM per device.

v0:
```python
import math

import jax
import jax.numpy as jnp
from jax import lax
from jax.sharding import PartitionSpec as P

N = 2048
SP = 16


def split_up(array, dim, peers):
    before, after = (array.shape[:dim], array.shape[dim + 1 :])
    return jnp.moveaxis(array.reshape(*before, peers, -1, *after), dim, 0)


def laid_out(parts, dim):
    parts = jnp.moveaxis(parts, 0, dim)
    lengths = parts.shape
    return parts.reshape(*lengths[:dim], lengths[dim] * lengths[dim + 1], *lengths[dim + 2 :])


def one_exchange(array, axis, axes, splits, concats):
    sizes = [lax.axis_size(a) for a in axes]
    parts = split_up(array, splits[0], sizes[0])
    parts = jnp.moveaxis(split_up(parts, splits[1] + 1, sizes[1]), 0, 1)
    inside = parts.shape[2:]
    parts = parts.reshape(-1, *inside)
    parts = lax.all_to_all(parts, axis, split_axis=0, concat_axis=0, tiled=True)
    parts = laid_out(parts.reshape(*sizes, *inside), concats[0] + 1)
    return laid_out(parts, concats[1])


def circle(count, period, width):
    first_ids = jnp.arange(count, dtype=jnp.int32)
    second_ids = jnp.arange(width, dtype=jnp.int32)
    phases = first_ids[:, None] * second_ids[None, :] % period
    angles = phases.astype(jnp.float32) * (2.0 * math.pi / period)
    return (jnp.cos(angles), jnp.sin(angles))


def mixed(form, left, right):
    return jnp.einsum(form, left, right, precision=lax.Precision.HIGHEST)


def spectral(real_in, imag_in):
    length = real_in.shape[-1]
    first = 32
    second = length // first
    shape_lead = real_in.shape[:-1]
    cos_first, sin_first = circle(first, first, first)
    cos_twist, sin_twist = circle(first, length, second)
    cos_second, sin_second = circle(second, second, second)
    grid_re = real_in.reshape(shape_lead + (first, second))
    section_re = mixed("...ab,ac->...cb", grid_re, cos_first)
    section_im = mixed("...ab,ac->...cb", grid_re, sin_first)
    grid_im = imag_in.reshape(shape_lead + (first, second))
    section_re = section_re - mixed("...ab,ac->...cb", grid_im, sin_first)
    section_im = section_im + mixed("...ab,ac->...cb", grid_im, cos_first)
    twist_re = section_re * cos_twist - section_im * sin_twist
    twist_im = section_re * sin_twist + section_im * cos_twist
    final_re = mixed("...cb,bd->...dc", twist_re, cos_second) - mixed(
        "...cb,bd->...dc", twist_im, sin_second
    )
    final_im = mixed("...cb,bd->...dc", twist_re, sin_second) + mixed(
        "...cb,bd->...dc", twist_im, cos_second
    )
    return (final_re.reshape(shape_lead + (length,)), final_im.reshape(shape_lead + (length,)))


def spectral_lead(real_in):
    row_total, length = real_in.shape
    first = 32
    second = length // first
    cos_first, sin_first = circle(first, first, first)
    cos_twist, sin_twist = circle(first, length, second)
    cos_second, sin_second = circle(second, second, second)
    grid_re = real_in.reshape(row_total, first, second)
    section_re = mixed("rab,ac->cbr", grid_re, cos_first)
    section_im = mixed("rab,ac->cbr", grid_re, sin_first)
    twist_re = section_re * cos_twist[:, :, None] - section_im * sin_twist[:, :, None]
    twist_im = section_re * sin_twist[:, :, None] + section_im * cos_twist[:, :, None]
    final_re = mixed("cbr,bd->dcr", twist_re, cos_second) - mixed(
        "cbr,bd->dcr", twist_im, sin_second
    )
    final_im = mixed("cbr,bd->dcr", twist_re, sin_second) + mixed(
        "cbr,bd->dcr", twist_im, cos_second
    )
    return (final_re.reshape(length, row_total), final_im.reshape(length, row_total))


def keep_map(first_coords, second_coords, radius_table, levels):
    node_count = radius_table.shape[1]
    first_node = (first_coords + SP // 2) // SP
    first_dist = first_coords - SP * first_node
    second_node = (second_coords + SP // 2) // SP
    second_dist = second_coords - SP * second_node
    plane_node = (levels + SP // 2) // SP
    plane_dist = levels - SP * plane_node
    node_ids = jnp.arange(node_count, dtype=jnp.int32)
    pick_first = (first_node[:, None] == node_ids[None, :]).astype(jnp.bfloat16)
    pick_second = (second_node[:, None] == node_ids[None, :]).astype(jnp.bfloat16)
    table_half = jnp.einsum(
        "hn,snm->shm",
        pick_first,
        radius_table.astype(jnp.bfloat16),
        preferred_element_type=jnp.float32,
    ).astype(jnp.bfloat16)
    plane_radius = jnp.einsum(
        "shm,km->shk", table_half, pick_second, preferred_element_type=jnp.float32
    )
    level_ids = jnp.arange(radius_table.shape[0], dtype=jnp.int32)
    pick_plane = (plane_node[:, None] == level_ids[None, :]).astype(jnp.float32)
    radius = jnp.einsum("ls,shk->hlk", pick_plane, plane_radius, precision=lax.Precision.HIGHEST)
    distance = (
        (first_dist * first_dist)[:, None, None]
        + (plane_dist * plane_dist)[None, :, None]
        + (second_dist * second_dist)[None, None, :]
    )
    return (distance.astype(jnp.float32) >= radius).astype(jnp.float32)


def body(intensity, punch_radius):
    row_count = lax.axis_size("row")
    col_count = lax.axis_size("col")
    row_at = lax.axis_index("row")
    col_at = lax.axis_index("col")
    planes, h_block, k_block = intensity.shape
    groups = col_count // row_count
    fine_width = k_block // col_count
    pencil_rows = groups * fine_width
    levels = jnp.arange(planes, dtype=jnp.int32)
    swapped_table = jnp.swapaxes(punch_radius, 1, 2)
    outgoing = jnp.transpose(
        intensity.reshape(planes, h_block, col_count, fine_width), (2, 3, 0, 1)
    )
    arrived = lax.all_to_all(
        lax.all_to_all(outgoing, "col", split_axis=0, concat_axis=0, tiled=True),
        "row",
        split_axis=0,
        concat_axis=3,
        tiled=True,
    )
    pencil_h = (
        h_block * row_at
        + k_block * jnp.arange(groups, dtype=jnp.int32)[:, None]
        + fine_width * col_at
        + jnp.arange(fine_width, dtype=jnp.int32)[None, :]
    ).reshape(-1)
    whole_k = jnp.arange(N, dtype=jnp.int32)
    mirrored = arrived.reshape(pencil_rows, planes, N)
    pencil_input = jnp.transpose(
        intensity.reshape(planes, groups, col_count, fine_width, k_block), (1, 2, 3, 0, 4)
    )
    direct = lax.all_to_all(pencil_input, "col", split_axis=1, concat_axis=4, tiled=True).reshape(
        pencil_rows, planes, N
    )
    keep_mask = keep_map(pencil_h, whole_k, punch_radius, levels)
    keep_swap = keep_map(pencil_h, whole_k, swapped_table, levels)
    counts = jnp.maximum(keep_mask + keep_swap, 1.0)
    symmetric = ((keep_mask * direct + keep_swap * mirrored) / counts).astype(jnp.bfloat16)
    row_total = pencil_rows * planes
    flat_rows = symmetric.reshape(row_total, N).astype(jnp.float32)
    part_re, part_im = spectral_lead(flat_rows)
    freq_width = N // (row_count * col_count)
    sectioned = jnp.stack([part_re, part_im]).reshape(
        2, row_count, col_count, freq_width, row_total
    )
    spectra = one_exchange(sectioned, ("row", "col"), ("row", "col"), (1, 2), (1, 2))
    spectra = spectra.reshape(2, row_count, col_count, freq_width, groups, fine_width, planes)
    spectra = jnp.transpose(spectra, (0, 6, 3, 1, 4, 2, 5)).reshape(2, planes * freq_width, N)
    final_re, final_im = spectral(spectra[0], spectra[1])
    out_re = (final_re / N).reshape(planes, freq_width, N)
    out_im = (final_im / N).reshape(planes, freq_width, N)
    return (out_re, out_im)


def solution(mesh):
    in_specs = (P(None, "row", "col"), P())
    out_specs = (P(None, ("row", "col"), None), P(None, ("row", "col"), None))
    return jax.shard_map(body, mesh=mesh, in_specs=in_specs, out_specs=out_specs, check_vma=False)
```

profile of v0, /device:TPU:1, one launch (start us, length us, event | category | flops | bytes accessed | tf_op | source)
XLA Modules:
  0.0 269.4 jit_solution(14947244395660178085)
XLA Ops:
  0.6 2.9 %copy.76 = f32[16,256,64]{1,0,2:T(8,128)} copy(f32[16,256,64]{1,2,0:T(8,128)} %param.2) | data formatting | bytes 2097152 | tf_op args[0]
  3.5 11.2 %all-to-all-start.1 = ((f32[32,2,16,256]{3,2,1,0:T(8,128)}), f32[32,2,16,256]{3,2,1,0:T(8,128)}, u32[]{:S(2)}, u32[]{:S(2)}) async-start(f32[32,2,16,256]{3,2,1,0:T(8,128)} %bitcast.15), calls=%async_computation.1 | async-start | bytes 2097152 | tf_op jit(solution)/shard_map/all_to_all | solution.py:138
  14.7 2.5 copy.71
  17.2 1.8 copy.131
  19.1 2.3 reshape.326
  21.3 19.9 %all-to-all-done.1 = f32[32,2,16,256]{3,2,1,0:T(8,128)} async-done(((f32[32,2,16,256]{3,2,1,0:T(8,128)}), f32[32,2,16,256]{3,2,1,0:T(8,128)}, u32[]{:S(2)}, u32[]{:S(2)}) %all-to-all-start.1) | async-done | bytes 1048608 | tf_op jit(solution)/shard_map/all_to_all | solution.py:138
  41.2 6.0 %all-to-all-start = ((f32[32,1,8192]{2,1,0:T(1,128)}), f32[32,1,8192]{2,1,0:T(1,128)S(1)}, u32[]{:S(2)}, u32[]{:S(2)}) async-start(f32[32,1,8192]{2,1,0:T(1,128)} %reshape.326), calls=%async_computation | async-start | bytes 2097152 | tf_op jit(solution)/shard_map/all_to_all | solution.py:155
  48.0 25.7 %all-to-all-done = f32[32,1,8192]{2,1,0:T(1,128)S(1)} async-done(((f32[32,1,8192]{2,1,0:T(1,128)}), f32[32,1,8192]{2,1,0:T(1,128)S(1)}, u32[]{:S(2)}, u32[]{:S(2)}) %all-to-all-start) | async-done | bytes 1048608 | tf_op jit(solution)/shard_map/all_to_all | solution.py:155
  73.7 6.5 %all-to-all-start.2 = ((f32[32,2,16,256]{3,2,1,0:T(8,128)}), f32[32,2,16,256]{3,2,1,0:T(8,128)}, u32[]{:S(2)}, u32[]{:S(2)}) async-start(f32[32,2,16,256]{3,2,1,0:T(8,128)} %all-to-all-done.1), calls=%async_computation.2 | async-start | bytes 2097152 | tf_op jit(solution)/shard_map/all_to_all | solution.py:137
  82.8 3.2 %reduce = f32[32,8192]{1,0:T(8,128)S(1)} reduce(f32[32,1,8192]{2,1,0:T(1,128)S(1)} %all-to-all-done, f32[]{:T(128)} %broadcast.588), dimensions={1}, to_apply=%all_to_all.28.reduce_sub_computation | reduce | bytes 2097156 | tf_op jit(solution)/shard_map/all_to_all | solution.py:155
  89.0 8.5 %all-to-all-done.2 = f32[32,2,16,256]{3,2,1,0:T(8,128)} async-done(((f32[32,2,16,256]{3,2,1,0:T(8,128)}), f32[32,2,16,256]{3,2,1,0:T(8,128)}, u32[]{:S(2)}, u32[]{:S(2)}) %all-to-all-start.2) | async-done | bytes 1048608 | tf_op jit(solution)/shard_map/all_to_all | solution.py:137
  97.5 1.8 copy.77
  99.5 2.1 divide_convert_fusion
  106.1 1.7 fusion.21
  107.8 1.6 fusion.23
  109.4 1.7 convolution_subtract_fusion.2
  111.1 1.7 convolution_add_fusion.2
  114.4 60.7 %all_to_all.40 = f32[256,2,1,1,8,128]{5,4,1,3,2,0:T(8,128)S(1)} all-to-all(f32[256,2,1,1,8,128]{5,4,1,3,2,0:T(8,128)S(1)} %copy.86), channel_id=1, replica_groups=mesh['row'=8,'col'=32] {'row','col'}, dimensions={0} | all-to-all | bytes 4194304 | tf_op jit(solution)/shard_map/all_to_all | solution.py:29
  175.1 4.6 %copy.87 = f32[2,8,32,1,8,128]{2,5,4,1,0,3:T(8,128)} copy(f32[2,8,32,1,8,128]{5,4,0,2,1,3:T(8,128)S(1)} %bitcast.141) | data formatting | bytes 4194304 | tf_op jit(solution)/shard_map/transpose | solution.py:18
  179.7 8.6 %fusion.168 = (f32[1,16,8,8,4,32,2]{5,1,6,4,2,3,0:T(8,128)}, f32[1,16,8,8,4,32,2]{5,1,6,4,2,3,0:T(8,128)}) fusion(f32[2,16,8,8,4,32,2]{5,1,6,4,2,3,0:T(8,128)} %bitcast.140), kind=kLoop, calls=%fused_computation.192 | loop fusion | bytes 4194304 | tf_op jit(solution)/shard_map/slice | solution.py:172
  188.3 14.0 %copy.100 = f32[1,16,8,8,4,32,2]{2,1,4,3,6,5,0:T(8,128)} copy(f32[1,16,8,8,4,32,2]{5,1,6,4,2,3,0:T(8,128)} %get-tuple-element.5) | data formatting | bytes 2097152 | tf_op jit(solution)/shard_map/reshape;squeeze | solution.py:54
  202.3 11.8 %reshape.324 = f32[128,32,64]{0,1,2:T(8,128)S(1)} reshape(f32[1,16,8,8,4,32,2]{2,1,4,3,6,5,0:T(8,128)} %copy.100) | data formatting | bytes 2097152 | tf_op jit(solution)/shard_map/reshape;squeeze | solution.py:54
  216.2 14.0 %copy.101 = f32[1,16,8,8,4,32,2]{2,1,4,3,6,5,0:T(8,128)} copy(f32[1,16,8,8,4,32,2]{5,1,6,4,2,3,0:T(8,128)} %get-tuple-element.4) | data formatting | bytes 2097152 | tf_op jit(solution)/shard_map/reshape;squeeze | solution.py:57
  230.2 11.9 %reshape.325 = f32[128,32,64]{0,1,2:T(8,128)S(1)} reshape(f32[1,16,8,8,4,32,2]{2,1,4,3,6,5,0:T(8,128)} %copy.101) | data formatting | bytes 2097152 | tf_op jit(solution)/shard_map/reshape;squeeze | solution.py:57
  244.8 1.7 fusion.15
  246.5 1.6 fusion.17
  248.1 1.7 fusion.5
  249.8 1.7 fusion.3
  251.5 4.4 %copy.99 = f32[128,64,32]{2,1,0:T(8,128)} copy(f32[128,64,32]{0,1,2:T(8,128)S(1)} %fusion.3) | data formatting | bytes 2097152 | tf_op jit(solution)/shard_map/div | solution.py:174
  255.9 4.4 %div.101 = f32[16,8,2048]{2,1,0:T(8,128)} reshape(f32[128,64,32]{2,1,0:T(8,128)} %copy.99) | data formatting | bytes 2097152 | tf_op jit(solution)/shard_map/div | solution.py:174
  260.3 4.4 %copy.96 = f32[128,64,32]{2,1,0:T(8,128)} copy(f32[128,64,32]{0,1,2:T(8,128)S(1)} %fusion.5) | data formatting | bytes 2097152 | tf_op jit(solution)/shard_map/div | solution.py:173
  264.8 4.4 %div.98 = f32[16,8,2048]{2,1,0:T(8,128)} reshape(f32[128,64,32]{2,1,0:T(8,128)} %copy.96) | data formatting | bytes 2097152 | tf_op jit(solution)/shard_map/div | solution.py:173
  (37 shorter events, 17.2 us)
Async XLA Ops:
  0.6 14.1 %copy-start = (f32[16,256,64]{1,2,0:T(8,128)S(1)}, f32[16,256,64]{1,2,0:T(8,128)}, u32[]{:S(2)}) copy-start(f32[16,256,64]{1,2,0:T(8,128)} %param.2) | copy-start | bytes 3145732
  3.5 37.7 %all-to-all-start.1 = ((f32[32,2,16,256]{3,2,1,0:T(8,128)}), f32[32,2,16,256]{3,2,1,0:T(8,128)}, u32[]{:S(2)}, u32[]{:S(2)}) async-start(f32[32,2,16,256]{3,2,1,0:T(8,128)} %bitcast.15), calls=%async_computation.1 | async-start | bytes 2097152 | tf_op jit(solution)/shard_map/all_to_all | solution.py:138
  19.1 28.5 %copy-start.1 = (s32[2,129,129]{2,0,1:T(2,128)S(1)}, s32[2,129,129]{2,0,1:T(2,128)}, u32[]{:S(2)}) copy-start(s32[2,129,129]{2,0,1:T(2,128)} %param.3) | copy-start | bytes 399388
  41.2 32.5 %all-to-all-start = ((f32[32,1,8192]{2,1,0:T(1,128)}), f32[32,1,8192]{2,1,0:T(1,128)S(1)}, u32[]{:S(2)}, u32[]{:S(2)}) async-start(f32[32,1,8192]{2,1,0:T(1,128)} %reshape.326), calls=%async_computation | async-start | bytes 2097152 | tf_op jit(solution)/shard_map/all_to_all | solution.py:155
  73.7 23.8 %all-to-all-start.2 = ((f32[32,2,16,256]{3,2,1,0:T(8,128)}), f32[32,2,16,256]{3,2,1,0:T(8,128)}, u32[]{:S(2)}, u32[]{:S(2)}) async-start(f32[32,2,16,256]{3,2,1,0:T(8,128)} %all-to-all-done.1), calls=%async_computation.2 | async-start | bytes 2097152 | tf_op jit(solution)/shard_map/all_to_all | solution.py:137
where the time goes:
time: 274 us; the launch traced here: 269 us
  local copies, waits for them, and re-layouts  102 us (37%)
  blocking collectives  60.7 us (22%)
  waiting for transfers between devices  54.1 us (20%)
  matrix products  24.2 us (9%)
  starting transfers between devices  23.7 us (9%)
  other arithmetic  3.92 us (1%)
    all_to_all x1, blocking collectives, one_exchange(): parts = lax.all_to_all(parts, axis, split_axis=0, concat_axis=0, tiled=True)  60.7 us
    another operation x2, local copies, waits for them, and re-layouts, spectral(): grid_im = imag_in.reshape(shape_lead + (first, second))  25.9 us
    another operation x2, local copies, waits for them, and re-layouts, spectral(): grid_re = real_in.reshape(shape_lead + (first, second))  25.7 us
    all_to_all x1, waiting for transfers between devices, body(): lax.all_to_all(pencil_input, 'col', split_axis=1, concat_axis=4, tiled=True)  25.7 us
    all_to_all x1, waiting for transfers between devices, body(): lax.all_to_all(outgoing, 'col', split_axis=0, concat_axis=0, tiled=True)  19.9 us
    dot_general x14, matrix products, mixed(): return jnp.einsum(form, left, right, precision=lax.Precision.HIGHEST)  19.9 us
    all_to_all x1, starting transfers between devices, body(): lax.all_to_all(outgoing, 'col', split_axis=0, concat_axis=0, tiled=True)  11.2 us
    div x2, local copies, waits for them, and re-layouts, body(): out_im = (final_im / N).reshape(planes, freq_width, N)  8.88 us
  transfers between devices with their start and end apart: 3, of which 3 were waited for; matrix products, arithmetic and copies ran while one was open for 6% of the time, Pallas kernels for 0%

commit v1 on v0

v1 whole, which is shorter than its diff:
```python
import functools

import jax
import jax.numpy as jnp
import ml_dtypes
import numpy as np
from jax import lax
from jax.experimental import pallas as pl
from jax.experimental.pallas import tpu as pltpu
from jax.sharding import PartitionSpec as P

N = 2048
SP = 16
PLANES = 16
CLASSES = 16
OWN = N // CLASSES
LANES = 128
TOP = 6.0
CODE = 32700.0 / TOP**0.25
BF = jnp.bfloat16
F32 = jnp.float32


def dot(left, right, contract=(1, 0)):
    dims = (((contract[0],), (contract[1],)), ((), ()))
    return lax.dot_general(left, right, dims, preferred_element_type=F32)


def split_table(table):
    high = table.astype(ml_dtypes.bfloat16)
    low = (table - high.astype(np.float64)).astype(ml_dtypes.bfloat16)
    return high, low


def wave(phases, period):
    angles = 2.0 * np.pi * (phases % period) / period
    return np.cos(angles), np.sin(angles)


def encode_kernel(step_planes, at_ref, table_ref, x_ref, out_ref, g_ref, e_ref, t_ref):
    step = pl.program_id(0)
    half = LANES // 2

    @pl.when(step == 0)
    def _():
        row_at, col_at = at_ref[0], at_ref[1]
        rows = lax.broadcasted_iota(jnp.int32, (256, 256), 0)
        nodes = lax.broadcasted_iota(jnp.int32, (256, 256), 1)
        pick_h = ((256 * row_at + rows + SP // 2) // SP == nodes).astype(F32).astype(BF)
        sub = lax.broadcasted_iota(jnp.int32, (256, LANES), 0)
        lane = lax.broadcasted_iota(jnp.int32, (256, LANES), 1)
        same = (64 * col_at + lane % half + SP // 2) // SP == sub
        pick_low = (same & (lane < half)).astype(F32).astype(BF)
        pick_high = (same & (lane >= half)).astype(F32).astype(BF)
        off_h = (lax.broadcasted_iota(jnp.int32, (128, LANES), 0) + SP // 2) % SP - SP // 2
        off_k = (lax.broadcasted_iota(jnp.int32, (128, LANES), 1) + SP // 2) % SP - SP // 2
        near = (off_h * off_h + off_k * off_k).astype(F32)
        for s in range(2):
            for side in range(2):
                left = dot(pick_h, table_ref[s], (1, side)).astype(BF)
                radius = dot(left[:128], pick_low) + dot(left[128:], pick_high)
                g_ref[2 * s + side] = radius - near

    for i in range(step_planes):
        level = step * step_planes + i
        node = (level + SP // 2) // SP
        off = level - SP * node
        far = (off * off).astype(F32)
        x = x_ref[i]
        packed = jnp.concatenate([x[:128], x[128:]], axis=1)
        keep = far >= g_ref[2 * node]
        swap = far >= g_ref[2 * node + 1]
        value = jnp.where(keep, packed * jnp.where(swap, 0.5, 1.0), 0.0)
        size = lax.rsqrt(lax.rsqrt(jnp.abs(value))) * CODE + 0.5
        size = size.astype(jnp.int32)
        code = jnp.where(value < 0.0, -size, size)
        e_ref[i] = code
        t_ref[i] = code.T
        for m in range(CLASSES):
            direct = t_ref[i, pl.ds(m, 8, stride=CLASSES), :]
            mirror = e_ref[i, pl.ds(m, 8, stride=CLASSES), :]
            out_ref[i * CLASSES + m] = jnp.concatenate([direct, mirror], axis=0).astype(jnp.int16)


def encode(at, table, intensity):
    planes, h_block, k_block = intensity.shape
    step_planes = 4
    steps = planes // step_planes
    count = step_planes * CLASSES
    return pl.pallas_call(
        functools.partial(encode_kernel, step_planes),
        grid=(steps,),
        in_specs=[
            pl.BlockSpec(memory_space=pltpu.SMEM),
            pl.BlockSpec((2, 256, 256), lambda i: (0, 0, 0)),
            pl.BlockSpec((step_planes, h_block, k_block), lambda i: (i, 0, 0)),
        ],
        out_specs=pl.BlockSpec((count, 16, LANES), lambda i: (i, 0, 0)),
        out_shape=jax.ShapeDtypeStruct((planes * CLASSES, 16, LANES), jnp.int16),
        scratch_shapes=[
            pltpu.VMEM((4, 128, LANES), F32),
            pltpu.VMEM((step_planes, 128, LANES), jnp.int32),
            pltpu.VMEM((step_planes, 128, LANES), jnp.int32),
        ],
        compiler_params=pltpu.CompilerParams(vmem_limit_bytes=24 << 20),
    )(at, table, intensity)


def decoded(codes):
    u = codes.astype(jnp.int32).astype(F32) * (1.0 / CODE)
    return (u * u) * (u * jnp.abs(u))


def times(re, im, c, s):
    return re * c - im * s, re * s + im * c


def four(a, b, c, d):
    s_re, s_im = a[0] + c[0], a[1] + c[1]
    d_re, d_im = a[0] - c[0], a[1] - c[1]
    t_re, t_im = b[0] + d[0], b[1] + d[1]
    e_re, e_im = b[0] - d[0], b[1] - d[1]
    return (
        (s_re + t_re, s_im + t_im),
        (d_re - e_im, d_im + e_re),
        (s_re - t_re, s_im - t_im),
        (d_re + e_im, d_im - e_re),
    )


def eight(y):
    even = four(y[0], y[2], y[4], y[6])
    odd = four(y[1], y[3], y[5], y[7])
    root = float(np.sqrt(0.5))
    o1 = ((odd[1][0] - odd[1][1]) * root, (odd[1][0] + odd[1][1]) * root)
    o2 = (-odd[2][1], odd[2][0])
    o3 = (-(odd[3][0] + odd[3][1]) * root, (odd[3][0] - odd[3][1]) * root)
    odd = (odd[0], o1, o2, o3)
    first = [(e[0] + o[0], e[1] + o[1]) for e, o in zip(even, odd)]
    second = [(e[0] - o[0], e[1] - o[1]) for e, o in zip(even, odd)]
    return first + second


def column_kernel(codes_ref, dft_ref, cos_ref, sin_ref, out_ref, s_ref, y_ref):
    sub = lax.broadcasted_iota(jnp.int32, (16, 8, LANES), 1)
    lane = lax.broadcasted_iota(jnp.int32, (8, 8, LANES), 2)
    for tile in range(N // LANES):
        row, upper = tile // 2, tile % 2
        got = decoded(codes_ref[32 * row : 32 * row + 32])[:, :8].reshape(16, 2, 8, LANES)
        even, odd = got[:, 0], got[:, 1]
        if upper:
            direct = jnp.where(sub < 4, pltpu.roll(even, 4, 1), odd)
        else:
            direct = jnp.where(sub < 4, even, pltpu.roll(odd, 4, 1))
        pair = [
            jnp.stack([decoded(codes_ref[32 * r + 2 * tile + j])[8:] for r in range(8)])
            for j in range(2)
        ]
        low = jnp.where(lane < 64, pair[0], pltpu.roll(pair[1], 64, 2))
        high = jnp.where(lane < 64, pltpu.roll(pair[0], 64, 2), pair[1])
        mirror = jnp.stack([low, high], axis=1)
        whole = direct.reshape(128, LANES) + mirror.reshape(128, LANES)
        s_ref[tile * LANES : (tile + 1) * LANES, :] = whole.T
    right = jnp.concatenate(
        [s_ref[pl.ds(a, 256, stride=8), :].astype(BF) for a in range(8)], axis=1
    )
    y_ref[...] = dot(dft_ref[...], jnp.concatenate([right, right], axis=0))

    def block(i, carry):
        at = pl.multiple_of(i * 8, 8)
        y = []
        for a in range(8):
            lanes = slice(a * LANES, (a + 1) * LANES)
            re = y_ref[pl.ds(at, 8), lanes]
            im = y_ref[pl.ds(256 + at, 8), lanes]
            if a:
                re, im = times(re, im, cos_ref[pl.ds(at, 8), lanes], sin_ref[pl.ds(at, 8), lanes])
            y.append((re, im))
        for c, (re, im) in enumerate(eight(y)):
            out_ref[32 * c + i] = jnp.concatenate([re, im], axis=0).astype(BF)
        return carry

    lax.fori_loop(0, 32, block, 0)


def column_tables():
    d = np.arange(256)
    cos, sin = wave(d[:, None] * d[None, :], 256)
    high, low = split_table(np.concatenate([cos, sin], axis=0))
    dft = np.concatenate([high, low], axis=1)
    cos, sin = wave(d[:, None] * np.repeat(np.arange(8), LANES)[None, :], N)
    return dft, cos.astype(np.float32), sin.astype(np.float32)


def columns(codes):
    vmem = pl.BlockSpec(memory_space=pltpu.VMEM)
    return pl.pallas_call(
        column_kernel,
        in_specs=[vmem] * 4,
        out_specs=vmem,
        out_shape=jax.ShapeDtypeStruct((256, 16, LANES), BF),
        scratch_shapes=[pltpu.VMEM((N, LANES), F32), pltpu.VMEM((512, 8 * LANES), F32)],
        compiler_params=pltpu.CompilerParams(vmem_limit_bytes=40 << 20),
    )(codes, *map(jnp.asarray, column_tables()))


def sixteen(y):
    first = [four(y[i], y[i + 4], y[i + 8], y[i + 12]) for i in range(4)]
    out = [None] * 16
    for k in range(4):
        turned = []
        for i in range(4):
            re, im = first[i][k]
            if i * k:
                angle = 2.0 * np.pi * i * k / 16
                c, s = float(np.cos(angle)), float(np.sin(angle))
                if i * k == 4:
                    re, im = -im, re
                elif i * k == 2:
                    re, im = (re - im) * c, (re + im) * c
                elif i * k == 6:
                    re, im = -(re + im) * s, (re - im) * s
                else:
                    re, im = times(re, im, c, s)
            turned.append((re, im))
        for j, value in enumerate(four(*turned)):
            out[k + 4 * j] = value
    return out


def row_kernel(step_planes, x_ref, dft_ref, cos_ref, sin_ref, re_ref, im_ref, y_ref):
    for i in range(step_planes):
        x = x_ref[CLASSES * i : CLASSES * (i + 1)].reshape(CLASSES * 16, LANES)
        y_ref[i] = dot(jnp.concatenate([x, x], axis=1), dft_ref[...])
        y = []
        for m in range(CLASSES):
            real, imag = slice(16 * m, 16 * m + 8), slice(16 * m + 8, 16 * m + 16)
            re = y_ref[i, real, :LANES] - y_ref[i, imag, LANES:]
            im = y_ref[i, real, LANES:] + y_ref[i, imag, :LANES]
            if m:
                re, im = times(re, im, cos_ref[m : m + 1], sin_ref[m : m + 1])
            y.append((re, im))
        for d, (re, im) in enumerate(sixteen(y)):
            re_ref[i, :, d * LANES : (d + 1) * LANES] = re
            im_ref[i, :, d * LANES : (d + 1) * LANES] = im


def row_tables():
    t = np.arange(LANES)
    cos, sin = wave(t[:, None] * t[None, :], LANES)
    high, low = split_table(np.concatenate([cos, sin], axis=1) / N)
    cos, sin = wave(np.arange(CLASSES)[:, None] * t[None, :], N)
    return np.concatenate([high, low], axis=0), cos.astype(np.float32), sin.astype(np.float32)


def rows(spectra):
    step_planes = 4
    block = pl.BlockSpec((step_planes, 8, N), lambda i: (i, 0, 0))
    shape = jax.ShapeDtypeStruct((PLANES, 8, N), F32)
    return pl.pallas_call(
        functools.partial(row_kernel, step_planes),
        grid=(PLANES // step_planes,),
        in_specs=[
            pl.BlockSpec((step_planes * CLASSES, 16, LANES), lambda i: (i, 0, 0)),
            pl.BlockSpec((2 * LANES, 2 * LANES), lambda i: (0, 0)),
            pl.BlockSpec((CLASSES, LANES), lambda i: (0, 0)),
            pl.BlockSpec((CLASSES, LANES), lambda i: (0, 0)),
        ],
        out_specs=[block, block],
        out_shape=[shape, shape],
        scratch_shapes=[pltpu.VMEM((step_planes, 256, 256), F32)],
        compiler_params=pltpu.CompilerParams(vmem_limit_bytes=40 << 20),
    )(spectra, *map(jnp.asarray, row_tables()))


def exchange(array):
    return lax.all_to_all(array, ("row", "col"), split_axis=0, concat_axis=0, tiled=True)


def body(intensity, punch_radius):
    at = jnp.stack([lax.axis_index("row"), lax.axis_index("col")]).astype(jnp.int32)
    nodes = punch_radius.shape[1]
    table = jnp.pad(punch_radius.astype(BF), ((0, 0), (0, 256 - nodes), (0, 256 - nodes)))
    codes = exchange(encode(at, table, intensity))
    spectra = exchange(columns(codes))
    return tuple(rows(spectra))


def solution(mesh):
    in_specs = (P(None, "row", "col"), P())
    out_specs = (P(None, ("row", "col"), None), P(None, ("row", "col"), None))
    return jax.shard_map(body, mesh=mesh, in_specs=in_specs, out_specs=out_specs, check_vma=False)
```

time: 274 us -> 95.6 us (0.35); the launches traced: 269 us -> 95.4 us
  local copies, waits for them, and re-layouts: 102 us -> 1.91 us
  waiting for transfers between devices: 54.1 us -> 0 us
  matrix products: 24.2 us -> 0 us
  starting transfers between devices: 23.7 us -> 0 us
  blocking collectives: 60.7 us -> 83.8 us
  Pallas kernels: 0 us -> 7.84 us
  other arithmetic: 3.92 us -> 1.12 us
    all_to_all x3 -> x0, waiting for transfers between devices: 54.1 us -> none  [the longest x1 25.7 us: body(): lax.all_to_all(pencil_input, 'col', split_axis=1, concat_axis=4, tiled=True)]
    another operation x4 -> x0, local copies, waits for them, and re-layouts: 51.7 us -> none  [the longest x2 25.9 us: spectral(): grid_im = imag_in.reshape(shape_lead + (first, second))]
    dot_general x18 -> x0, matrix products: 24.2 us -> none  [the longest x14 19.9 us: mixed(): return jnp.einsum(form, left, right, precision=lax.Precision.HIGHEST)]
    all_to_all x3 -> x0, starting transfers between devices: 23.7 us -> none  [the longest x1 11.2 us: body(): lax.all_to_all(outgoing, 'col', split_axis=0, concat_axis=0, tiled=True)]
    all_to_all x1 -> x2, blocking collectives: 60.7 us -> 83.8 us  [exchange(): lax.all_to_all(array, ('row', 'col'), split_axis=0, concat_axis=0, tiled=...]
    div x4 -> x0, local copies, waits for them, and re-layouts: 17.8 us -> none  [the longest x2 8.88 us: body(): out_im = (final_im / N).reshape(planes, freq_width, N)]
    slice x1 -> x0, local copies, waits for them, and re-layouts: 8.55 us -> none  [body(): final_re, final_im = spectral(spectra[0], spectra[1])]
    pallas_call x0 -> x3, Pallas kernels: none -> 7.84 us  [the longest x1 2.85 us: encode(): pl.pallas_call(functools.partial(encode_kernel, step_planes), grid=(steps...]
  transfers between devices with their start and end apart: 3 -> 0, of which waited for: 3 -> 0; matrix products, arithmetic and copies ran while one was open for 6% -> 0% of each run, Pallas kernels for 0% -> 0%
where the time goes in v1:
time: 95.6 us; the launch traced here: 95.4 us
  blocking collectives  83.8 us (88%)
  Pallas kernels  7.84 us (8%)
  local copies, waits for them, and re-layouts  1.91 us (2%)
  other arithmetic  1.12 us (1%)
    all_to_all x2, blocking collectives, exchange(): lax.all_to_all(array, ('row', 'col'), split_axis=0, concat_axis=0, tiled=...  83.8 us
    pallas_call x1, Pallas kernels, encode(): pl.pallas_call(functools.partial(encode_kernel, step_planes), grid=(steps...  2.85 us
    pallas_call x1, Pallas kernels, rows(): pl.pallas_call(functools.partial(row_kernel, step_planes), grid=(PLANES /...  2.71 us
    pallas_call x1, Pallas kernels, columns(): pl.pallas_call(column_kernel, in_specs=[vmem] * 4, out_specs=vmem, out_sh...  2.28 us

profile of v1, /device:TPU:1, one launch (start us, length us, event | category | flops | bytes accessed | tf_op | source)
XLA Modules:
  0.0 95.4 jit_solution(17313162691212722420)
XLA Ops:
  0.6 1.0 %convert_element_type.5 = bf16[2,129,129]{2,0,1:T(2,128)(2,1)S(1)} convert(s32[2,129,129]{2,0,1:T(2,128)} %param.9) | non-fusion elementwise | flops 33282 | bytes 199692 | tf_op jit(solution)/shard_map/convert_element_type | solution.py:283
  1.7 1.8 %copy.13.x_ref = f32[16,256,64]{2,1,0:T(8,128)S(1)} copy(f32[16,256,64]{1,2,0:T(8,128)} %param.8) | data formatting | bytes 2097152 | tf_op args[0]
  3.5 0.1 pad_add_fusion.at_ref
  3.7 0.0 copy-start
  3.7 0.0 copy-start.1
  3.7 0.0 copy-start.2
  3.7 2.8 %shard_map.95 = s16[256,16,128]{2,1,0:T(8,128)(2,1)S(1)} custom-call(s32[2]{0:T(128)S(1)} %pad_add_fusion.at_ref, bf16[2,256,256]{2,1,0:T(8,128)(2,1)S(1)} %pad.4.table_ref, f32[16,256,64]{2,1,0:T(8,128)S(1)} %copy.13.x_ref), custom_call_target="tpu_custom_call" | custom-call | tf_op jit(solution)/shard_map/pallas_call | solution.py:90
  6.5 46.4 %all_to_all.10.codes_ref = s16[256,16,128]{2,1,0:T(8,128)(2,1)S(1)} all-to-all(s16[256,16,128]{2,1,0:T(8,128)(2,1)S(1)} %shard_map.95), channel_id=1, replica_groups=mesh['row'=8,'col'=32] {'row','col'}, dimensions={0} | all-to-all | bytes 2097152 | tf_op jit(solution)/shard_map/all_to_all | solution.py:277
  53.0 0.0 copy-done
  53.0 0.0 copy-done.1
  53.0 0.0 copy-done.2
  53.0 2.3 %shard_map.96 = bf16[256,16,128]{2,1,0:T(8,128)(2,1)S(1)} custom-call(s16[256,16,128]{2,1,0:T(8,128)(2,1)S(1)} %all_to_all.10.codes_ref, bf16[512,512]{1,0:T(8,128)(2,1)S(1)} %copy-done.2, f32[256,1024]{1,0:T(8,128)S(1)} %copy-done.1, f32[256,1024]{1,0:T(8,128)S(1)} %copy-done), custom_call_target="tpu_custom_call" | custom-call | tf_op jit(solution)/shard_map/pallas_call | solution.py:197
  55.3 0.0 copy-start.3
  55.3 0.0 copy-start.4
  55.3 0.0 copy-start.5
  55.3 37.3 %all_to_all.11.x_ref = bf16[256,16,128]{2,1,0:T(8,128)(2,1)S(1)} all-to-all(bf16[256,16,128]{2,1,0:T(8,128)(2,1)S(1)} %shard_map.96), channel_id=1, replica_groups=mesh['row'=8,'col'=32] {'row','col'}, dimensions={0} | all-to-all | bytes 2097152 | tf_op jit(solution)/shard_map/all_to_all | solution.py:277
  92.6 0.0 copy-done.3
  92.7 0.0 copy-done.4
  92.7 0.0 copy-done.5
  92.7 2.7 %shard_map.97 = (f32[16,8,2048]{2,1,0:T(8,128)}, f32[16,8,2048]{2,1,0:T(8,128)}) custom-call(bf16[256,16,128]{2,1,0:T(8,128)(2,1)S(1)} %all_to_all.11.x_ref, bf16[256,256]{1,0:T(8,128)(2,1)S(1)} %copy-done.3, f32[16,128]{1,0:T(8,128)S(1)} %copy-done.5, f32[16,128]{1,0:T(8,128)S(1)} %copy-done.4), custom_call_target="tpu_custom_call" | custom-call | tf_op jit(solution)/shard_map/pallas_call | solution.py:260
  (2 shorter events, 0.0 us)
Async XLA Ops:
  3.7 49.3 %copy-start = (f32[256,1024]{1,0:T(8,128)S(1)}, f32[256,1024]{1,0:T(8,128)}, u32[]{:S(2)}) copy-start(f32[256,1024]{1,0:T(8,128)} %constant.26.clone.sin_ref) | copy-start | bytes 3145732
  3.7 49.3 %copy-start.1 = (f32[256,1024]{1,0:T(8,128)S(1)}, f32[256,1024]{1,0:T(8,128)}, u32[]{:S(2)}) copy-start(f32[256,1024]{1,0:T(8,128)} %constant.25.clone.cos_ref) | copy-start | bytes 3145732
  3.7 49.3 %copy-start.2 = (bf16[512,512]{1,0:T(8,128)(2,1)S(1)}, bf16[512,512]{1,0:T(8,128)(2,1)}, u32[]{:S(2)}) copy-start(bf16[512,512]{1,0:T(8,128)(2,1)} %constant.24.clone.dft_ref) | copy-start | bytes 1572868
  55.3 37.4 %copy-start.3 = (bf16[256,256]{1,0:T(8,128)(2,1)S(1)}, bf16[256,256]{1,0:T(8,128)(2,1)}, u32[]{:S(2)}) copy-start(bf16[256,256]{1,0:T(8,128)(2,1)} %constant.27.clone.dft_ref) | copy-start | bytes 393220
  55.3 37.3 %copy-start.4 = (f32[16,128]{1,0:T(8,128)S(1)}, f32[16,128]{1,0:T(8,128)}, u32[]{:S(2)}) copy-start(f32[16,128]{1,0:T(8,128)} %constant.29.clone.sin_ref) | copy-start | bytes 24580
  55.3 37.3 %copy-start.5 = (f32[16,128]{1,0:T(8,128)S(1)}, f32[16,128]{1,0:T(8,128)}, u32[]{:S(2)}) copy-start(f32[16,128]{1,0:T(8,128)} %constant.28.clone.cos_ref) | copy-start | bytes 24580

commit v2 on v1

v2 whole, which is shorter than its diff:
```python
import jax
import jax.numpy as jnp
import ml_dtypes
import numpy as np
from jax import lax
from jax.experimental import pallas as pl
from jax.experimental.pallas import tpu as pltpu
from jax.sharding import PartitionSpec as P

N = 2048
SP = 16
PLANES = 16
CLASSES = 16
OWN = N // CLASSES
LANES = 128
TOP = 6.0
CODE = 32700.0 / TOP**0.25
BF = jnp.bfloat16
F32 = jnp.float32


def dot(left, right, contract=(1, 0)):
    dims = (((contract[0],), (contract[1],)), ((), ()))
    return lax.dot_general(left, right, dims, preferred_element_type=F32)


def split_table(table):
    high = table.astype(ml_dtypes.bfloat16)
    low = (table - high.astype(np.float64)).astype(ml_dtypes.bfloat16)
    return high, low


def wave(phases, period):
    angles = 2.0 * np.pi * (phases % period) / period
    return np.cos(angles), np.sin(angles)


def encode_kernel(x_hbm, table_hbm, out_hbm, code_ref, x_ref, near_h, near_k, g_ref, e_ref, t_ref, sems):
    half = LANES // 2
    row_at, col_at = lax.axis_index("row"), lax.axis_index("col")
    across, down = near_h.shape[0], near_k.shape[0]
    tables = [
        pltpu.make_async_copy(table_hbm.at[pl.ds(16 * row_at, across)], near_h, sems.at[4]),
        pltpu.make_async_copy(table_hbm.at[pl.ds(4 * col_at, down)], near_k, sems.at[5]),
    ]
    chunks = [
        pltpu.make_async_copy(x_hbm.at[pl.ds(4 * j, 4)], x_ref.at[pl.ds(4 * j, 4)], sems.at[j])
        for j in range(4)
    ]
    for copy in tables + chunks:
        copy.start()

    def picks(shape, base):
        places = lax.broadcasted_iota(jnp.int32, shape, 0)
        nodes = lax.broadcasted_iota(jnp.int32, shape, 1)
        return ((base + places + SP // 2) // SP == nodes).astype(F32).astype(BF)

    h_any, k_any = picks((256, table_hbm.shape[2]), 256 * row_at), picks((64, table_hbm.shape[2]), 64 * col_at)
    h_own, k_own = picks((256, across), 0), picks((64, down), 0)
    off_h = (lax.broadcasted_iota(jnp.int32, (64, 256), 1) + SP // 2) % SP - SP // 2
    off_k = (lax.broadcasted_iota(jnp.int32, (64, 256), 0) + SP // 2) % SP - SP // 2
    near = (off_h * off_h + off_k * off_k).astype(F32)
    for copy in tables:
        copy.wait()
    for s in range(2):
        keep = dot(k_any, near_h[:, s, :].astype(F32).astype(BF), (1, 1)).astype(BF)
        keep = dot(keep, h_own, (1, 1)) - near
        swap = dot(k_own, near_k[:, s, :].astype(F32).astype(BF)).astype(BF)
        swap = dot(swap, h_any, (1, 1)) - near
        for side, g in enumerate((keep, swap)):
            g_ref[2 * s + side] = jnp.concatenate([g[:, :128], g[:, 128:]], axis=0)

    def plane(level, node, far):
        x = x_ref[level]
        packed = jnp.concatenate([x[:, :128], x[:, 128:]], axis=0)
        keep = far >= g_ref[2 * node]
        swap = far >= g_ref[2 * node + 1]
        value = jnp.where(keep, packed * jnp.where(swap, 0.5, 1.0), 0.0)
        size = lax.rsqrt(lax.rsqrt(jnp.abs(value))) * CODE + 0.5
        size = size.astype(jnp.int32)
        code = jnp.where(value < 0.0, -size, size)
        t_ref[level] = code
        e_ref[level] = code.T
        for m in range(CLASSES):
            direct = t_ref[level, pl.ds(m, 8, stride=CLASSES), :]
            mirror = e_ref[level, pl.ds(m, 8, stride=CLASSES), :]
            both = jnp.concatenate([direct, mirror], axis=0).astype(jnp.int16)
            code_ref[level * CLASSES + m] = both

    sent = []
    for j in range(4):
        chunks[j].wait()
        for level in range(4 * j, 4 * j + 4):
            node = (level + SP // 2) // SP
            plane(level, node, float((level - SP * node) ** 2))
        part = pl.ds(4 * CLASSES * j, 4 * CLASSES)
        copy = pltpu.make_async_copy(code_ref.at[part], out_hbm.at[part], sems.at[6 + j])
        copy.start()
        sent.append(copy)
    for copy in sent:
        copy.wait()


def encode(intensity, punch_radius):
    planes, h_block, k_block = intensity.shape
    hbm = pl.BlockSpec(memory_space=pltpu.HBM)
    across, down, nodes = h_block // SP + 1, k_block // SP + 1, punch_radius.shape[2]
    return pl.pallas_call(
        encode_kernel,
        in_specs=[hbm, hbm],
        out_specs=hbm,
        out_shape=jax.ShapeDtypeStruct((planes * CLASSES, 16, LANES), jnp.int16),
        scratch_shapes=[
            pltpu.VMEM((planes * CLASSES, 16, LANES), jnp.int16),
            pltpu.VMEM((planes, k_block, h_block), F32),
            pltpu.VMEM((across, 2, nodes), jnp.int32),
            pltpu.VMEM((down, 2, nodes), jnp.int32),
            pltpu.VMEM((4, 128, LANES), F32),
            pltpu.VMEM((planes, 128, LANES), jnp.int32),
            pltpu.VMEM((planes, 128, LANES), jnp.int32),
            pltpu.SemaphoreType.DMA((10,)),
        ],
        compiler_params=pltpu.CompilerParams(vmem_limit_bytes=58 << 20),
    )(jnp.swapaxes(intensity, 1, 2), jnp.swapaxes(punch_radius, 0, 1))


def decoded(codes):
    u = codes.astype(jnp.int32).astype(F32) * (1.0 / CODE)
    return (u * u) * (u * jnp.abs(u))


def times(re, im, c, s):
    return re * c - im * s, re * s + im * c


def four(a, b, c, d):
    s_re, s_im = a[0] + c[0], a[1] + c[1]
    d_re, d_im = a[0] - c[0], a[1] - c[1]
    t_re, t_im = b[0] + d[0], b[1] + d[1]
    e_re, e_im = b[0] - d[0], b[1] - d[1]
    return (
        (s_re + t_re, s_im + t_im),
        (d_re - e_im, d_im + e_re),
        (s_re - t_re, s_im - t_im),
        (d_re + e_im, d_im - e_re),
    )


def eight(y):
    even = four(y[0], y[2], y[4], y[6])
    odd = four(y[1], y[3], y[5], y[7])
    root = float(np.sqrt(0.5))
    o1 = ((odd[1][0] - odd[1][1]) * root, (odd[1][0] + odd[1][1]) * root)
    o2 = (-odd[2][1], odd[2][0])
    o3 = (-(odd[3][0] + odd[3][1]) * root, (odd[3][0] - odd[3][1]) * root)
    odd = (odd[0], o1, o2, o3)
    first = [(e[0] + o[0], e[1] + o[1]) for e, o in zip(even, odd)]
    second = [(e[0] - o[0], e[1] - o[1]) for e, o in zip(even, odd)]
    return first + second


def column_kernel(codes_ref, order_ref, dft_ref, cos_ref, sin_ref, out_ref, s_ref, y_ref):
    sub = lax.broadcasted_iota(jnp.int32, (16, 8, LANES), 1)
    lane = lax.broadcasted_iota(jnp.int32, (8, 8, LANES), 2)
    for tile in range(N // LANES):
        row, upper = tile // 2, tile % 2
        got = decoded(codes_ref[32 * row : 32 * row + 32])[:, :8].reshape(16, 2, 8, LANES)
        even, odd = got[:, 0], got[:, 1]
        if upper:
            direct = jnp.where(sub < 4, pltpu.roll(even, 4, 1), odd)
        else:
            direct = jnp.where(sub < 4, even, pltpu.roll(odd, 4, 1))
        pair = [
            jnp.stack([decoded(codes_ref[32 * r + 2 * tile + j])[8:] for r in range(8)])
            for j in range(2)
        ]
        low = jnp.where(lane < 64, pair[0], pltpu.roll(pair[1], 64, 2))
        high = jnp.where(lane < 64, pltpu.roll(pair[0], 64, 2), pair[1])
        mirror = jnp.stack([low, high], axis=1)
        whole = (direct.reshape(128, LANES) + mirror.reshape(128, LANES)).astype(BF)
        turned = dot(order_ref[...], whole, (1, 1)).astype(BF)
        for a in range(8):
            lanes = slice(a * LANES, (a + 1) * LANES)
            s_ref[16 * tile : 16 * tile + 16, lanes] = turned[16 * a : 16 * a + 16]
    right = s_ref[...]
    right = jnp.concatenate([right, right], axis=0)
    for part in range(2):
        y_ref[256 * part : 256 * part + 256] = dot(dft_ref[256 * part : 256 * part + 256], right)
    for i in range(32):
        y = []
        for a in range(8):
            lanes = slice(a * LANES, (a + 1) * LANES)
            at = slice(8 * i, 8 * i + 8)
            here = 8 * i + i // 16 * 128
            re, im = y_ref[here : here + 8, lanes], y_ref[here + 128 : here + 136, lanes]
            if a:
                re, im = times(re, im, cos_ref[at, lanes], sin_ref[at, lanes])
            y.append((re, im))
        for c, (re, im) in enumerate(eight(y)):
            out_ref[32 * c + i] = jnp.concatenate([re, im], axis=0).astype(BF)


def column_tables():
    d = np.arange(256)
    cos, sin = wave(d[:, None] * d[None, :], 256)
    order = [cos[:128], sin[:128], cos[128:], sin[128:]]
    high, low = split_table(np.concatenate(order, axis=0))
    dft = np.concatenate([high, low], axis=1)
    cos, sin = wave(d[:, None] * np.repeat(np.arange(8), LANES)[None, :], N)
    order = np.zeros((LANES, LANES))
    order[np.arange(LANES), np.arange(LANES) % 16 * 8 + np.arange(LANES) // 16] = 1.0
    return order.astype(ml_dtypes.bfloat16), dft, cos.astype(np.float32), sin.astype(np.float32)


def columns(codes):
    vmem = pl.BlockSpec(memory_space=pltpu.VMEM)
    return pl.pallas_call(
        column_kernel,
        in_specs=[vmem] * 5,
        out_specs=vmem,
        out_shape=jax.ShapeDtypeStruct((256, 16, LANES), BF),
        scratch_shapes=[pltpu.VMEM((256, 8 * LANES), BF), pltpu.VMEM((512, 8 * LANES), F32)],
        compiler_params=pltpu.CompilerParams(vmem_limit_bytes=40 << 20),
    )(codes, *map(jnp.asarray, column_tables()))


def sixteen(y):
    first = [four(y[i], y[i + 4], y[i + 8], y[i + 12]) for i in range(4)]
    out = [None] * 16
    for k in range(4):
        turned = []
        for i in range(4):
            re, im = first[i][k]
            if i * k:
                angle = 2.0 * np.pi * i * k / 16
                c, s = float(np.cos(angle)), float(np.sin(angle))
                if i * k == 4:
                    re, im = -im, re
                elif i * k == 2:
                    re, im = (re - im) * c, (re + im) * c
                elif i * k == 6:
                    re, im = -(re + im) * s, (re - im) * s
                else:
                    re, im = times(re, im, c, s)
            turned.append((re, im))
        for j, value in enumerate(four(*turned)):
            out[k + 4 * j] = value
    return out


def row_kernel(x_ref, dft_ref, cos_ref, sin_ref, re_hbm, im_hbm, re_ref, im_ref, y_ref, sems):
    copies = []

    def matmul(i):
        x = x_ref[CLASSES * i : CLASSES * (i + 1)].reshape(CLASSES * 16, LANES)
        y_ref[i] = dot(jnp.concatenate([x, x], axis=1), dft_ref[...])

    matmul(0)
    for i in range(PLANES):
        if i + 1 < PLANES:
            matmul(i + 1)
        y = []
        for m in range(CLASSES):
            real, imag = slice(16 * m, 16 * m + 8), slice(16 * m + 8, 16 * m + 16)
            re = y_ref[i, real, :LANES] - y_ref[i, imag, LANES:]
            im = y_ref[i, real, LANES:] + y_ref[i, imag, :LANES]
            if m:
                re, im = times(re, im, cos_ref[m : m + 1], sin_ref[m : m + 1])
            y.append((re, im))
        for d, (re, im) in enumerate(sixteen(y)):
            re_ref[i, :, d * LANES : (d + 1) * LANES] = re
            im_ref[i, :, d * LANES : (d + 1) * LANES] = im
        if i % 2:
            done = pl.ds(i - 1, 2)
            pairs = ((re_ref, re_hbm), (im_ref, im_hbm))
            for which, (here, there) in enumerate(pairs):
                copy = pltpu.make_async_copy(here.at[done], there.at[done], sems.at[i // 2, which])
                copy.start()
                copies.append(copy)
    for copy in copies:
        copy.wait()


def row_tables():
    t = np.arange(LANES)
    cos, sin = wave(t[:, None] * t[None, :], LANES)
    high, low = split_table(np.concatenate([cos, sin], axis=1) / N)
    cos, sin = wave(np.arange(CLASSES)[:, None] * t[None, :], N)
    return np.concatenate([high, low], axis=0), cos.astype(np.float32), sin.astype(np.float32)


def rows(spectra):
    vmem, hbm = pl.BlockSpec(memory_space=pltpu.VMEM), pl.BlockSpec(memory_space=pltpu.HBM)
    shape = jax.ShapeDtypeStruct((PLANES, 8, N), F32)
    return pl.pallas_call(
        row_kernel,
        in_specs=[vmem] * 4,
        out_specs=[hbm, hbm],
        out_shape=[shape, shape],
        scratch_shapes=[
            pltpu.VMEM((PLANES, 8, N), F32),
            pltpu.VMEM((PLANES, 8, N), F32),
            pltpu.VMEM((PLANES, 256, 256), F32),
            pltpu.SemaphoreType.DMA((PLANES // 2, 2)),
        ],
        compiler_params=pltpu.CompilerParams(vmem_limit_bytes=40 << 20),
    )(spectra, *map(jnp.asarray, row_tables()))


def exchange(array):
    return lax.all_to_all(array, ("row", "col"), split_axis=0, concat_axis=0, tiled=True)


def body(intensity, punch_radius):
    codes = exchange(encode(intensity, punch_radius))
    spectra = exchange(columns(codes))
    return tuple(rows(spectra))


def solution(mesh):
    in_specs = (P(None, "row", "col"), P())
    out_specs = (P(None, ("row", "col"), None), P(None, ("row", "col"), None))
    return jax.shard_map(body, mesh=mesh, in_specs=in_specs, out_specs=out_specs, check_vma=False)
```

time: 95.6 us -> 92 us (0.962)
  local copies, waits for them, and re-layouts: 1.91 us -> 0.05 us
  other arithmetic: 1.12 us -> 0 us
    unnamed x13 -> x14, local copies, waits for them, and re-layouts: 1.87 us -> 0.05 us
    convert_element_type x1 -> x0, other arithmetic: 1.04 us -> none  [body(): punch_radius.astype(BF)]
where the time goes in v2:
time: 92 us; the launch traced here: 91.8 us
  blocking collectives  84 us (91%)
  Pallas kernels  7.1 us (8%)
    all_to_all x2, blocking collectives, exchange(): lax.all_to_all(array, ('row', 'col'), split_axis=0, concat_axis=0, tiled=...  84 us
    pallas_call x1, Pallas kernels, encode(): pl.pallas_call(encode_kernel, in_specs=[hbm, hbm], out_specs=hbm, out_sha...  3.48 us

profile of v2, /device:TPU:1, one launch (start us, length us, event | category | flops | bytes accessed | tf_op | source)
XLA Modules:
  0.0 91.8 jit_solution(7095857624955070534)
XLA Ops:
  0.6 0.0 copy-start.2
  0.6 0.0 copy-start.4
  0.7 3.5 %shard_map.104 = s16[256,16,128]{2,1,0:T(8,128)(2,1)} custom-call(f32[16,64,256]{2,1,0:T(8,128)} %bitcast.2, s32[129,2,129]{2,1,0:T(2,128)} %bitcast.3), custom_call_target="tpu_custom_call" | custom-call | tf_op jit(solution)/shard_map/pallas_call | solution.py:108
  4.1 0.0 copy-start
  4.2 0.0 copy-start.1
  4.2 46.7 %all_to_all.10.codes_ref = s16[256,16,128]{2,1,0:T(8,128)(2,1)S(1)} all-to-all(s16[256,16,128]{2,1,0:T(8,128)(2,1)} %shard_map.104), channel_id=1, replica_groups=mesh['row'=8,'col'=32] {'row','col'}, dimensions={0} | all-to-all | bytes 2097152 | tf_op jit(solution)/shard_map/all_to_all | solution.py:311
  50.8 0.0 copy-done.2
  50.8 0.0 copy-done.4
  50.8 0.0 copy-done
  50.8 0.0 copy-done.1
  50.8 1.8 %shard_map.105 = bf16[256,16,128]{2,1,0:T(8,128)(2,1)S(1)} custom-call(s16[256,16,128]{2,1,0:T(8,128)(2,1)S(1)} %all_to_all.10.codes_ref, bf16[128,128]{1,0:T(8,128)(2,1)S(1)} %copy-done.4, bf16[512,512]{1,0:T(8,128)(2,1)S(1)} %copy-done.2, f32[256,1024]{1,0:T(8,128)S(1)} %copy-done.1, f32[256,1024]{1,0:T(8,128)S(1)} %copy-done), custom_call_target="tpu_custom_call" | custom-call | tf_op jit(solution)/shard_map/pallas_call | solution.py:217
  52.7 0.0 copy-start.3
  52.7 0.0 copy-start.5
  52.7 0.0 copy-start.6
  52.7 37.3 %all_to_all.11.x_ref = bf16[256,16,128]{2,1,0:T(8,128)(2,1)S(1)} all-to-all(bf16[256,16,128]{2,1,0:T(8,128)(2,1)S(1)} %shard_map.105), channel_id=1, replica_groups=mesh['row'=8,'col'=32] {'row','col'}, dimensions={0} | all-to-all | bytes 2097152 | tf_op jit(solution)/shard_map/all_to_all | solution.py:311
  90.0 0.0 copy-done.3
  90.0 0.0 copy-done.5
  90.0 0.0 copy-done.6
  90.0 1.8 %shard_map.106 = (f32[16,8,2048]{2,1,0:T(8,128)}, f32[16,8,2048]{2,1,0:T(8,128)}) custom-call(bf16[256,16,128]{2,1,0:T(8,128)(2,1)S(1)} %all_to_all.11.x_ref, bf16[256,256]{1,0:T(8,128)(2,1)S(1)} %copy-done.3, f32[16,128]{1,0:T(8,128)S(1)} %copy-done.6, f32[16,128]{1,0:T(8,128)S(1)} %copy-done.5), custom_call_target="tpu_custom_call" | custom-call | tf_op jit(solution)/shard_map/pallas_call | solution.py:295
Async XLA Ops:
  0.6 50.2 %copy-start.2 = (bf16[512,512]{1,0:T(8,128)(2,1)S(1)}, bf16[512,512]{1,0:T(8,128)(2,1)}, u32[]{:S(2)}) copy-start(bf16[512,512]{1,0:T(8,128)(2,1)} %constant.15.clone.dft_ref) | copy-start | bytes 1572868
  0.6 50.2 %copy-start.4 = (bf16[128,128]{1,0:T(8,128)(2,1)S(1)}, bf16[128,128]{1,0:T(8,128)(2,1)}, u32[]{:S(2)}) copy-start(bf16[128,128]{1,0:T(8,128)(2,1)} %constant.14.clone.order_ref) | copy-start | bytes 98308
  4.1 46.7 %copy-start = (f32[256,1024]{1,0:T(8,128)S(1)}, f32[256,1024]{1,0:T(8,128)}, u32[]{:S(2)}) copy-start(f32[256,1024]{1,0:T(8,128)} %constant.17.clone.sin_ref) | copy-start | bytes 3145732
  4.2 46.7 %copy-start.1 = (f32[256,1024]{1,0:T(8,128)S(1)}, f32[256,1024]{1,0:T(8,128)}, u32[]{:S(2)}) copy-start(f32[256,1024]{1,0:T(8,128)} %constant.16.clone.cos_ref) | copy-start | bytes 3145732
  52.7 37.4 %copy-start.3 = (bf16[256,256]{1,0:T(8,128)(2,1)S(1)}, bf16[256,256]{1,0:T(8,128)(2,1)}, u32[]{:S(2)}) copy-start(bf16[256,256]{1,0:T(8,128)(2,1)} %constant.18.clone.dft_ref) | copy-start | bytes 393220
  52.7 37.3 %copy-start.5 = (f32[16,128]{1,0:T(8,128)S(1)}, f32[16,128]{1,0:T(8,128)}, u32[]{:S(2)}) copy-start(f32[16,128]{1,0:T(8,128)} %constant.20.clone.sin_ref) | copy-start | bytes 24580
  52.7 37.3 %copy-start.6 = (f32[16,128]{1,0:T(8,128)S(1)}, f32[16,128]{1,0:T(8,128)}, u32[]{:S(2)}) copy-start(f32[16,128]{1,0:T(8,128)} %constant.19.clone.cos_ref) | copy-start | bytes 24580

commit v3 on v2

--- a/solution.py
+++ b/solution.py
@@ -35,7 +35,7 @@
     return np.cos(angles), np.sin(angles)
 
 
-def encode_kernel(x_hbm, table_hbm, out_hbm, code_ref, x_ref, near_h, near_k, g_ref, e_ref, t_ref, sems):
+def encode_kernel(x_hbm, table_hbm, code_ref, x_ref, near_h, near_k, g_ref, e_ref, t_ref, sems):
     half = LANES // 2
     row_at, col_at = lax.axis_index("row"), lax.axis_index("col")
     across, down = near_h.shape[0], near_k.shape[0]
@@ -87,18 +87,11 @@
             both = jnp.concatenate([direct, mirror], axis=0).astype(jnp.int16)
             code_ref[level * CLASSES + m] = both
 
-    sent = []
     for j in range(4):
         chunks[j].wait()
         for level in range(4 * j, 4 * j + 4):
             node = (level + SP // 2) // SP
             plane(level, node, float((level - SP * node) ** 2))
-        part = pl.ds(4 * CLASSES * j, 4 * CLASSES)
-        copy = pltpu.make_async_copy(code_ref.at[part], out_hbm.at[part], sems.at[6 + j])
-        copy.start()
-        sent.append(copy)
-    for copy in sent:
-        copy.wait()
 
 
 def encode(intensity, punch_radius):
@@ -108,17 +101,16 @@
     return pl.pallas_call(
         encode_kernel,
         in_specs=[hbm, hbm],
-        out_specs=hbm,
-        out_shape=jax.ShapeDtypeStruct((planes * CLASSES, 16, LANES), jnp.int16),
+        out_specs=pl.BlockSpec(memory_space=pltpu.VMEM),
+        out_shape=pltpu.VMEM((planes * CLASSES, 16, LANES), jnp.int16),
         scratch_shapes=[
-            pltpu.VMEM((planes * CLASSES, 16, LANES), jnp.int16),
             pltpu.VMEM((planes, k_block, h_block), F32),
             pltpu.VMEM((across, 2, nodes), jnp.int32),
             pltpu.VMEM((down, 2, nodes), jnp.int32),
             pltpu.VMEM((4, 128, LANES), F32),
             pltpu.VMEM((planes, 128, LANES), jnp.int32),
             pltpu.VMEM((planes, 128, LANES), jnp.int32),
-            pltpu.SemaphoreType.DMA((10,)),
+            pltpu.SemaphoreType.DMA((6,)),
         ],
         compiler_params=pltpu.CompilerParams(vmem_limit_bytes=58 << 20),
     )(jnp.swapaxes(intensity, 1, 2), jnp.swapaxes(punch_radius, 0, 1))
@@ -252,8 +244,10 @@
     copies = []
 
     def matmul(i):
-        x = x_ref[CLASSES * i : CLASSES * (i + 1)].reshape(CLASSES * 16, LANES)
-        y_ref[i] = dot(jnp.concatenate([x, x], axis=1), dft_ref[...])
+        x = x_ref[CLASSES * i : CLASSES * (i + 1)].astype(F32)
+        real = x[:, :8].reshape(CLASSES * 8, LANES).astype(BF)
+        imag = x[:, 8:].reshape(CLASSES * 8, LANES).astype(BF)
+        y_ref[i] = dot(jnp.concatenate([real, imag, real, imag], axis=1), dft_ref[...])
 
     matmul(0)
     for i in range(PLANES):
@@ -261,9 +255,7 @@
             matmul(i + 1)
         y = []
         for m in range(CLASSES):
-            real, imag = slice(16 * m, 16 * m + 8), slice(16 * m + 8, 16 * m + 16)
-            re = y_ref[i, real, :LANES] - y_ref[i, imag, LANES:]
-            im = y_ref[i, real, LANES:] + y_ref[i, imag, :LANES]
+            re, im = y_ref[i, 8 * m : 8 * m + 8, :LANES], y_ref[i, 8 * m : 8 * m + 8, LANES:]
             if m:
                 re, im = times(re, im, cos_ref[m : m + 1], sin_ref[m : m + 1])
             y.append((re, im))
@@ -284,7 +276,8 @@
 def row_tables():
     t = np.arange(LANES)
     cos, sin = wave(t[:, None] * t[None, :], LANES)
-    high, low = split_table(np.concatenate([cos, sin], axis=1) / N)
+    both = [np.concatenate([cos, sin], axis=1), np.concatenate([-sin, cos], axis=1)]
+    high, low = split_table(np.concatenate(both, axis=0) / N)
     cos, sin = wave(np.arange(CLASSES)[:, None] * t[None, :], N)
     return np.concatenate([high, low], axis=0), cos.astype(np.float32), sin.astype(np.float32)
 
@@ -300,7 +293,7 @@
         scratch_shapes=[
             pltpu.VMEM((PLANES, 8, N), F32),
             pltpu.VMEM((PLANES, 8, N), F32),
-            pltpu.VMEM((PLANES, 256, 256), F32),
+            pltpu.VMEM((PLANES, 128, 256), F32),
             pltpu.SemaphoreType.DMA((PLANES // 2, 2)),
         ],
         compiler_params=pltpu.CompilerParams(vmem_limit_bytes=40 << 20),

time: 92 us -> 91 us (0.989)
  no operation moved by 1% of the time
where the time goes in v3:
time: 91 us; the launch traced here: 90.8 us
  blocking collectives  83.8 us (92%)
  Pallas kernels  6.29 us (7%)
    all_to_all x2, blocking collectives, exchange(): lax.all_to_all(array, ('row', 'col'), split_axis=0, concat_axis=0, tiled=...  83.8 us
    pallas_call x1, Pallas kernels, encode(): pl.pallas_call(encode_kernel, in_specs=[hbm, hbm], out_specs=pl.BlockSpec...  2.73 us

profile of v3, /device:TPU:1, one launch (start us, length us, event | category | flops | bytes accessed | tf_op | source)
XLA Modules:
  0.0 90.8 jit_solution(6775064171402859676)
XLA Ops:
  0.6 0.0 copy-start.2
  0.6 0.0 copy-start.4
  0.7 2.7 %shard_map.104 = s16[256,16,128]{2,1,0:T(8,128)(2,1)S(1)} custom-call(f32[16,64,256]{2,1,0:T(8,128)} %bitcast.2, s32[129,2,129]{2,1,0:T(2,128)} %bitcast.3), custom_call_target="tpu_custom_call" | custom-call | tf_op jit(solution)/shard_map/pallas_call | solution.py:101
  3.4 0.0 copy-start
  3.4 0.0 copy-start.1
  3.4 46.4 %all_to_all.10.codes_ref = s16[256,16,128]{2,1,0:T(8,128)(2,1)S(1)} all-to-all(s16[256,16,128]{2,1,0:T(8,128)(2,1)S(1)} %shard_map.104), channel_id=1, replica_groups=mesh['row'=8,'col'=32] {'row','col'}, dimensions={0} | all-to-all | bytes 2097152 | tf_op jit(solution)/shard_map/all_to_all | solution.py:304
  49.9 0.0 copy-done.2
  49.9 0.0 copy-done.4
  49.9 0.0 copy-done
  49.9 0.0 copy-done.1
  49.9 1.8 %shard_map.105 = bf16[256,16,128]{2,1,0:T(8,128)(2,1)S(1)} custom-call(s16[256,16,128]{2,1,0:T(8,128)(2,1)S(1)} %all_to_all.10.codes_ref, bf16[128,128]{1,0:T(8,128)(2,1)S(1)} %copy-done.4, bf16[512,512]{1,0:T(8,128)(2,1)S(1)} %copy-done.2, f32[256,1024]{1,0:T(8,128)S(1)} %copy-done.1, f32[256,1024]{1,0:T(8,128)S(1)} %copy-done), custom_call_target="tpu_custom_call" | custom-call | tf_op jit(solution)/shard_map/pallas_call | solution.py:209
  51.7 0.0 copy-start.3
  51.7 0.0 copy-start.5
  51.7 0.0 copy-start.6
  51.7 37.3 %all_to_all.11.x_ref = bf16[256,16,128]{2,1,0:T(8,128)(2,1)S(1)} all-to-all(bf16[256,16,128]{2,1,0:T(8,128)(2,1)S(1)} %shard_map.105), channel_id=1, replica_groups=mesh['row'=8,'col'=32] {'row','col'}, dimensions={0} | all-to-all | bytes 2097152 | tf_op jit(solution)/shard_map/all_to_all | solution.py:304
  89.1 0.0 copy-done.3
  89.1 0.0 copy-done.5
  89.1 0.0 copy-done.6
  89.1 1.7 %shard_map.106 = (f32[16,8,2048]{2,1,0:T(8,128)}, f32[16,8,2048]{2,1,0:T(8,128)}) custom-call(bf16[256,16,128]{2,1,0:T(8,128)(2,1)S(1)} %all_to_all.11.x_ref, bf16[512,256]{1,0:T(8,128)(2,1)S(1)} %copy-done.3, f32[16,128]{1,0:T(8,128)S(1)} %copy-done.6, f32[16,128]{1,0:T(8,128)S(1)} %copy-done.5), custom_call_target="tpu_custom_call" | custom-call | tf_op jit(solution)/shard_map/pallas_call | solution.py:288
Async XLA Ops:
  0.6 49.2 %copy-start.2 = (bf16[512,512]{1,0:T(8,128)(2,1)S(1)}, bf16[512,512]{1,0:T(8,128)(2,1)}, u32[]{:S(2)}) copy-start(bf16[512,512]{1,0:T(8,128)(2,1)} %constant.15.clone.dft_ref) | copy-start | bytes 1572868
  0.6 49.2 %copy-start.4 = (bf16[128,128]{1,0:T(8,128)(2,1)S(1)}, bf16[128,128]{1,0:T(8,128)(2,1)}, u32[]{:S(2)}) copy-start(bf16[128,128]{1,0:T(8,128)(2,1)} %constant.14.clone.order_ref) | copy-start | bytes 98308
  3.4 46.5 %copy-start = (f32[256,1024]{1,0:T(8,128)S(1)}, f32[256,1024]{1,0:T(8,128)}, u32[]{:S(2)}) copy-start(f32[256,1024]{1,0:T(8,128)} %constant.17.clone.sin_ref) | copy-start | bytes 3145732
  3.4 46.5 %copy-start.1 = (f32[256,1024]{1,0:T(8,128)S(1)}, f32[256,1024]{1,0:T(8,128)}, u32[]{:S(2)}) copy-start(f32[256,1024]{1,0:T(8,128)} %constant.16.clone.cos_ref) | copy-start | bytes 3145732
  51.7 37.4 %copy-start.3 = (bf16[512,256]{1,0:T(8,128)(2,1)S(1)}, bf16[512,256]{1,0:T(8,128)(2,1)}, u32[]{:S(2)}) copy-start(bf16[512,256]{1,0:T(8,128)(2,1)} %constant.18.clone.dft_ref) | copy-start | bytes 786436
  51.7 37.3 %copy-start.5 = (f32[16,128]{1,0:T(8,128)S(1)}, f32[16,128]{1,0:T(8,128)}, u32[]{:S(2)}) copy-start(f32[16,128]{1,0:T(8,128)} %constant.20.clone.sin_ref) | copy-start | bytes 24580
  51.7 37.3 %copy-start.6 = (f32[16,128]{1,0:T(8,128)S(1)}, f32[16,128]{1,0:T(8,128)}, u32[]{:S(2)}) copy-start(f32[16,128]{1,0:T(8,128)} %constant.19.clone.cos_ref) | copy-start | bytes 24580

commit v4 on v3

--- a/solution.py
+++ b/solution.py
@@ -70,7 +70,9 @@
         for side, g in enumerate((keep, swap)):
             g_ref[2 * s + side] = jnp.concatenate([g[:, :128], g[:, 128:]], axis=0)
 
-    def plane(level, node, far):
+    def coded(level):
+        node = (level + SP // 2) // SP
+        far = float((level - SP * node) ** 2)
         x = x_ref[level]
         packed = jnp.concatenate([x[:, :128], x[:, 128:]], axis=0)
         keep = far >= g_ref[2 * node]
@@ -78,20 +80,20 @@
         value = jnp.where(keep, packed * jnp.where(swap, 0.5, 1.0), 0.0)
         size = lax.rsqrt(lax.rsqrt(jnp.abs(value))) * CODE + 0.5
         size = size.astype(jnp.int32)
-        code = jnp.where(value < 0.0, -size, size)
-        t_ref[level] = code
-        e_ref[level] = code.T
+        return jnp.where(value < 0.0, -size, size)
+
+    for pair in range(PLANES // 2):
+        if pair % 2 == 0:
+            chunks[pair // 2].wait()
+        word = (coded(2 * pair) << 16) | (coded(2 * pair + 1) & 0xFFFF)
+        t_ref[pair] = word
+        e_ref[pair] = word.T
         for m in range(CLASSES):
-            direct = t_ref[level, pl.ds(m, 8, stride=CLASSES), :]
-            mirror = e_ref[level, pl.ds(m, 8, stride=CLASSES), :]
-            both = jnp.concatenate([direct, mirror], axis=0).astype(jnp.int16)
-            code_ref[level * CLASSES + m] = both
-
-    for j in range(4):
-        chunks[j].wait()
-        for level in range(4 * j, 4 * j + 4):
-            node = (level + SP // 2) // SP
-            plane(level, node, float((level - SP * node) ** 2))
+            direct = t_ref[pair, pl.ds(m, 8, stride=CLASSES), :]
+            mirror = e_ref[pair, pl.ds(m, 8, stride=CLASSES), :]
+            both = jnp.concatenate([direct, mirror], axis=0)
+            code_ref[2 * pair * CLASSES + m] = (both >> 16).astype(jnp.int16)
+            code_ref[(2 * pair + 1) * CLASSES + m] = ((both << 16) >> 16).astype(jnp.int16)
 
 
 def encode(intensity, punch_radius):
@@ -108,8 +110,8 @@
             pltpu.VMEM((across, 2, nodes), jnp.int32),
             pltpu.VMEM((down, 2, nodes), jnp.int32),
             pltpu.VMEM((4, 128, LANES), F32),
-            pltpu.VMEM((planes, 128, LANES), jnp.int32),
-            pltpu.VMEM((planes, 128, LANES), jnp.int32),
+            pltpu.VMEM((planes // 2, 128, LANES), jnp.int32),
+            pltpu.VMEM((planes // 2, 128, LANES), jnp.int32),
             pltpu.SemaphoreType.DMA((6,)),
         ],
         compiler_params=pltpu.CompilerParams(vmem_limit_bytes=58 << 20),

time: 91 us -> 90.8 us (level)
  no operation moved by 1% of the time
where the time goes in v4:
time: 90.8 us; the launch traced here: 90.7 us
  blocking collectives  83.8 us (92%)
  Pallas kernels  6.16 us (7%)
    all_to_all x2, blocking collectives, exchange(): lax.all_to_all(array, ('row', 'col'), split_axis=0, concat_axis=0, tiled=...  83.8 us
    pallas_call x1, Pallas kernels, encode(): pl.pallas_call(encode_kernel, in_specs=[hbm, hbm], out_specs=pl.BlockSpec...  2.6 us

profile of v4, /device:TPU:1, one launch (start us, length us, event | category | flops | bytes accessed | tf_op | source)
XLA Modules:
  0.0 90.7 jit_solution(13988880569728340521)
XLA Ops:
  0.6 0.0 copy-start.2
  0.6 0.0 copy-start.4
  0.7 2.6 %shard_map.104 = s16[256,16,128]{2,1,0:T(8,128)(2,1)S(1)} custom-call(f32[16,64,256]{2,1,0:T(8,128)} %bitcast.2, s32[129,2,129]{2,1,0:T(2,128)} %bitcast.3), custom_call_target="tpu_custom_call" | custom-call | tf_op jit(solution)/shard_map/pallas_call | solution.py:103
  3.3 0.0 copy-start
  3.3 0.0 copy-start.1
  3.3 46.4 %all_to_all.10.codes_ref = s16[256,16,128]{2,1,0:T(8,128)(2,1)S(1)} all-to-all(s16[256,16,128]{2,1,0:T(8,128)(2,1)S(1)} %shard_map.104), channel_id=1, replica_groups=mesh['row'=8,'col'=32] {'row','col'}, dimensions={0} | all-to-all | bytes 2097152 | tf_op jit(solution)/shard_map/all_to_all | solution.py:306
  49.7 0.0 copy-done.2
  49.7 0.0 copy-done.4
  49.7 0.0 copy-done
  49.7 0.0 copy-done.1
  49.8 1.8 %shard_map.105 = bf16[256,16,128]{2,1,0:T(8,128)(2,1)S(1)} custom-call(s16[256,16,128]{2,1,0:T(8,128)(2,1)S(1)} %all_to_all.10.codes_ref, bf16[128,128]{1,0:T(8,128)(2,1)S(1)} %copy-done.4, bf16[512,512]{1,0:T(8,128)(2,1)S(1)} %copy-done.2, f32[256,1024]{1,0:T(8,128)S(1)} %copy-done.1, f32[256,1024]{1,0:T(8,128)S(1)} %copy-done), custom_call_target="tpu_custom_call" | custom-call | tf_op jit(solution)/shard_map/pallas_call | solution.py:211
  51.6 0.0 copy-start.3
  51.6 0.0 copy-start.5
  51.6 0.0 copy-start.6
  51.6 37.3 %all_to_all.11.x_ref = bf16[256,16,128]{2,1,0:T(8,128)(2,1)S(1)} all-to-all(bf16[256,16,128]{2,1,0:T(8,128)(2,1)S(1)} %shard_map.105), channel_id=1, replica_groups=mesh['row'=8,'col'=32] {'row','col'}, dimensions={0} | all-to-all | bytes 2097152 | tf_op jit(solution)/shard_map/all_to_all | solution.py:306
  88.9 0.0 copy-done.3
  88.9 0.0 copy-done.5
  88.9 0.0 copy-done.6
  88.9 1.7 %shard_map.106 = (f32[16,8,2048]{2,1,0:T(8,128)}, f32[16,8,2048]{2,1,0:T(8,128)}) custom-call(bf16[256,16,128]{2,1,0:T(8,128)(2,1)S(1)} %all_to_all.11.x_ref, bf16[512,256]{1,0:T(8,128)(2,1)S(1)} %copy-done.3, f32[16,128]{1,0:T(8,128)S(1)} %copy-done.6, f32[16,128]{1,0:T(8,128)S(1)} %copy-done.5), custom_call_target="tpu_custom_call" | custom-call | tf_op jit(solution)/shard_map/pallas_call | solution.py:290
Async XLA Ops:
  0.6 49.1 %copy-start.2 = (bf16[512,512]{1,0:T(8,128)(2,1)S(1)}, bf16[512,512]{1,0:T(8,128)(2,1)}, u32[]{:S(2)}) copy-start(bf16[512,512]{1,0:T(8,128)(2,1)} %constant.15.clone.dft_ref) | copy-start | bytes 1572868
  0.6 49.1 %copy-start.4 = (bf16[128,128]{1,0:T(8,128)(2,1)S(1)}, bf16[128,128]{1,0:T(8,128)(2,1)}, u32[]{:S(2)}) copy-start(bf16[128,128]{1,0:T(8,128)(2,1)} %constant.14.clone.order_ref) | copy-start | bytes 98308
  3.3 46.5 %copy-start = (f32[256,1024]{1,0:T(8,128)S(1)}, f32[256,1024]{1,0:T(8,128)}, u32[]{:S(2)}) copy-start(f32[256,1024]{1,0:T(8,128)} %constant.17.clone.sin_ref) | copy-start | bytes 3145732
  3.3 46.5 %copy-start.1 = (f32[256,1024]{1,0:T(8,128)S(1)}, f32[256,1024]{1,0:T(8,128)}, u32[]{:S(2)}) copy-start(f32[256,1024]{1,0:T(8,128)} %constant.16.clone.cos_ref) | copy-start | bytes 3145732
  51.6 37.4 %copy-start.3 = (bf16[512,256]{1,0:T(8,128)(2,1)S(1)}, bf16[512,256]{1,0:T(8,128)(2,1)}, u32[]{:S(2)}) copy-start(bf16[512,256]{1,0:T(8,128)(2,1)} %constant.18.clone.dft_ref) | copy-start | bytes 786436
  51.6 37.3 %copy-start.5 = (f32[16,128]{1,0:T(8,128)S(1)}, f32[16,128]{1,0:T(8,128)}, u32[]{:S(2)}) copy-start(f32[16,128]{1,0:T(8,128)} %constant.20.clone.sin_ref) | copy-start | bytes 24580
  51.6 37.3 %copy-start.6 = (f32[16,128]{1,0:T(8,128)S(1)}, f32[16,128]{1,0:T(8,128)}, u32[]{:S(2)}) copy-start(f32[16,128]{1,0:T(8,128)} %constant.19.clone.cos_ref) | copy-start | bytes 24580

commit v5 on v4

--- a/solution.py
+++ b/solution.py
@@ -13,8 +13,7 @@
 CLASSES = 16
 OWN = N // CLASSES
 LANES = 128
-TOP = 6.0
-CODE = 32700.0 / TOP**0.25
+CODE = 2.0**14.25
 BF = jnp.bfloat16
 F32 = jnp.float32
 
@@ -119,7 +118,7 @@
 
 
 def decoded(codes):
-    u = codes.astype(jnp.int32).astype(F32) * (1.0 / CODE)
+    u = codes.astype(jnp.int32).astype(F32)
     return (u * u) * (u * jnp.abs(u))
 
 
@@ -198,7 +197,7 @@
     d = np.arange(256)
     cos, sin = wave(d[:, None] * d[None, :], 256)
     order = [cos[:128], sin[:128], cos[128:], sin[128:]]
-    high, low = split_table(np.concatenate(order, axis=0))
+    high, low = split_table(np.concatenate(order, axis=0) * 2.0**-57)
     dft = np.concatenate([high, low], axis=1)
     cos, sin = wave(d[:, None] * np.repeat(np.arange(8), LANES)[None, :], N)
     order = np.zeros((LANES, LANES))

time: 90.8 us -> 90.8 us (level)
  no operation moved by 1% of the time
where the time goes in v5:
time: 90.8 us; the launch traced here: 90.6 us
  blocking collectives  83.8 us (92%)
  Pallas kernels  6.08 us (7%)
    all_to_all x2, blocking collectives, exchange(): lax.all_to_all(array, ('row', 'col'), split_axis=0, concat_axis=0, tiled=...  83.8 us
    pallas_call x1, Pallas kernels, encode(): pl.pallas_call(encode_kernel, in_specs=[hbm, hbm], out_specs=pl.BlockSpec...  2.6 us

profile of v5, /device:TPU:1, one launch (start us, length us, event | category | flops | bytes accessed | tf_op | source)
XLA Modules:
  0.0 90.6 jit_solution(11795943742407179928)
XLA Ops:
  0.6 0.0 copy-start.2
  0.6 0.0 copy-start.4
  0.7 2.6 %shard_map.104 = s16[256,16,128]{2,1,0:T(8,128)(2,1)S(1)} custom-call(f32[16,64,256]{2,1,0:T(8,128)} %bitcast.2, s32[129,2,129]{2,1,0:T(2,128)} %bitcast.3), custom_call_target="tpu_custom_call" | custom-call | tf_op jit(solution)/shard_map/pallas_call | solution.py:102
  3.3 0.0 copy-start
  3.3 0.0 copy-start.1
  3.3 46.4 %all_to_all.10.codes_ref = s16[256,16,128]{2,1,0:T(8,128)(2,1)S(1)} all-to-all(s16[256,16,128]{2,1,0:T(8,128)(2,1)S(1)} %shard_map.104), channel_id=1, replica_groups=mesh['row'=8,'col'=32] {'row','col'}, dimensions={0} | all-to-all | bytes 2097152 | tf_op jit(solution)/shard_map/all_to_all | solution.py:305
  49.7 0.0 copy-done.2
  49.7 0.0 copy-done.4
  49.7 0.0 copy-done
  49.7 0.0 copy-done.1
  49.8 1.7 %shard_map.105 = bf16[256,16,128]{2,1,0:T(8,128)(2,1)S(1)} custom-call(s16[256,16,128]{2,1,0:T(8,128)(2,1)S(1)} %all_to_all.10.codes_ref, bf16[128,128]{1,0:T(8,128)(2,1)S(1)} %copy-done.4, bf16[512,512]{1,0:T(8,128)(2,1)S(1)} %copy-done.2, f32[256,1024]{1,0:T(8,128)S(1)} %copy-done.1, f32[256,1024]{1,0:T(8,128)S(1)} %copy-done), custom_call_target="tpu_custom_call" | custom-call | tf_op jit(solution)/shard_map/pallas_call | solution.py:210
  51.5 0.0 copy-start.3
  51.5 0.0 copy-start.5
  51.5 0.0 copy-start.6
  51.5 37.3 %all_to_all.11.x_ref = bf16[256,16,128]{2,1,0:T(8,128)(2,1)S(1)} all-to-all(bf16[256,16,128]{2,1,0:T(8,128)(2,1)S(1)} %shard_map.105), channel_id=1, replica_groups=mesh['row'=8,'col'=32] {'row','col'}, dimensions={0} | all-to-all | bytes 2097152 | tf_op jit(solution)/shard_map/all_to_all | solution.py:305
  88.9 0.0 copy-done.3
  88.9 0.0 copy-done.5
  88.9 0.0 copy-done.6
  88.9 1.7 %shard_map.106 = (f32[16,8,2048]{2,1,0:T(8,128)}, f32[16,8,2048]{2,1,0:T(8,128)}) custom-call(bf16[256,16,128]{2,1,0:T(8,128)(2,1)S(1)} %all_to_all.11.x_ref, bf16[512,256]{1,0:T(8,128)(2,1)S(1)} %copy-done.3, f32[16,128]{1,0:T(8,128)S(1)} %copy-done.6, f32[16,128]{1,0:T(8,128)S(1)} %copy-done.5), custom_call_target="tpu_custom_call" | custom-call | tf_op jit(solution)/shard_map/pallas_call | solution.py:289
Async XLA Ops:
  0.6 49.1 %copy-start.2 = (bf16[512,512]{1,0:T(8,128)(2,1)S(1)}, bf16[512,512]{1,0:T(8,128)(2,1)}, u32[]{:S(2)}) copy-start(bf16[512,512]{1,0:T(8,128)(2,1)} %constant.15.clone.dft_ref) | copy-start | bytes 1572868
  0.6 49.1 %copy-start.4 = (bf16[128,128]{1,0:T(8,128)(2,1)S(1)}, bf16[128,128]{1,0:T(8,128)(2,1)}, u32[]{:S(2)}) copy-start(bf16[128,128]{1,0:T(8,128)(2,1)} %constant.14.clone.order_ref) | copy-start | bytes 98308
  3.3 46.5 %copy-start = (f32[256,1024]{1,0:T(8,128)S(1)}, f32[256,1024]{1,0:T(8,128)}, u32[]{:S(2)}) copy-start(f32[256,1024]{1,0:T(8,128)} %constant.17.clone.sin_ref) | copy-start | bytes 3145732
  3.3 46.5 %copy-start.1 = (f32[256,1024]{1,0:T(8,128)S(1)}, f32[256,1024]{1,0:T(8,128)}, u32[]{:S(2)}) copy-start(f32[256,1024]{1,0:T(8,128)} %constant.16.clone.cos_ref) | copy-start | bytes 3145732
  51.5 37.4 %copy-start.3 = (bf16[512,256]{1,0:T(8,128)(2,1)S(1)}, bf16[512,256]{1,0:T(8,128)(2,1)}, u32[]{:S(2)}) copy-start(bf16[512,256]{1,0:T(8,128)(2,1)} %constant.18.clone.dft_ref) | copy-start | bytes 786436
  51.5 37.3 %copy-start.5 = (f32[16,128]{1,0:T(8,128)S(1)}, f32[16,128]{1,0:T(8,128)}, u32[]{:S(2)}) copy-start(f32[16,128]{1,0:T(8,128)} %constant.20.clone.sin_ref) | copy-start | bytes 24580
  51.5 37.3 %copy-start.6 = (f32[16,128]{1,0:T(8,128)S(1)}, f32[16,128]{1,0:T(8,128)}, u32[]{:S(2)}) copy-start(f32[16,128]{1,0:T(8,128)} %constant.19.clone.cos_ref) | copy-start | bytes 24580
